TPU v7x, 32 devices: a whole 2x2x4 slice. The times are simulated.
32 devices in a mesh: groups: 2 (over y), frames: 4 (over z), fsdp: 2 (over x), heads: 2 (over core).
Axes of the slice: x: 2, y: 2, z: 4, core: 2. Of those that a mesh axis runs over, the one named last changes fastest.
Arguments:
- frames_in: bfloat16 [4, 768, 1536], P(('groups', 'fsdp'), 'frames', 'heads'), parts along dimension 0, may hold values from -6 to 6
- lengths: int32 [4], P(('groups', 'fsdp')), parts along dimension 0, may hold values from 192 to 768, as said below
- w_query: bfloat16 [1536, 768], P(('frames', 'fsdp'), 'heads')
- w_key: bfloat16 [1536, 768], P(('frames', 'fsdp'), 'heads'), may hold values from -0.15625 to 0.15625
- w_value: bfloat16 [1536, 768], P(('frames', 'fsdp'), 'heads'), may hold values from -0.15625 to 0.15625
- w_out: bfloat16 [768, 1536], P('heads', ('frames', 'fsdp')), may hold values from -0.21875 to 0.21875
- w_glu: bfloat16 [1536, 2, 1536], P('fsdp', None, 'heads'), may hold values from -0.15625 to 0.15625
- dw_kernel: bfloat16 [31, 1536], P(None, 'heads'), may hold values from -1 to 1
- w_pw: bfloat16 [1536, 1536], P('heads', 'fsdp'), may hold values from -0.15625 to 0.15625
Outputs:
- block_out: bfloat16 [4, 768, 1536], P(('groups', 'fsdp'), 'frames', 'heads'), parts along dimension 0
There are 2 independent parts, one for each index of `groups`. A program takes and returns all parts, laid end to end along the dimension named above; an argument that names none is the same for every part. Nothing has to cross between parts.
Inputs may be any that keep to these rules, and one draw needn't show every extreme that they name: `lengths`: each utterance counts at least 192 valid frames, and in every group some utterance is valid over all 768 frames.
All inputs are finite; a program needn't handle non-finite values.
Results may differ from a plain program's by a relative error of at most 0.012.
The roundings to bfloat16 on the way count: a program that leaves them out, or rounds other values in their place, can miss the bound.
Values may be sent and summed in bfloat16 or wider, within the bound.
A program may use at most 64 MiB of HBM per device.

v0:
```python
import math

import jax
import jax.numpy as jnp
from jax import lax
from jax.sharding import PartitionSpec as P

HEAD_DIM = 96
KERNEL = 31


EPS = 1e-05
NEG_FILL = -1e30


def padded_2(cells, sides, width):
    for axis, dim in sides:
        count = lax.axis_size(axis)
        ends = count - 1
        head = lax.slice_in_dim(cells, 0, width, axis=dim)
        tail = lax.slice_in_dim(cells, cells.shape[dim] - width, cells.shape[dim], axis=dim)
        cells = jnp.concatenate(
            [
                lax.ppermute(tail, axis, [(i, (i + 1) % count) for i in range(ends)]),
                cells,
                lax.ppermute(head, axis, [((i + 1) % count, i) for i in range(ends)]),
            ],
            axis=dim,
        )
    return cells


def layer_norm(rows):
    values = rows.astype(jnp.float32)
    mean_row = jnp.mean(values, axis=-1, keepdims=True)
    centred = values - mean_row
    variance = jnp.mean(centred * centred, axis=-1, keepdims=True)
    return centred * lax.rsqrt(variance + EPS)


def shards(frames_in, lengths, w_query, w_key, w_value, w_out, w_glu, dw_kernel, w_pw):
    full_rows = lax.all_gather(frames_in, "heads", axis=2, tiled=True)[0]
    frame_count = full_rows.shape[0]
    half_width = frames_in.shape[2]
    own_start = lax.axis_index("heads") * half_width
    normed = layer_norm(full_rows).astype(jnp.bfloat16)
    att_cols = w_query.shape[1]
    pieces = (
        lax.all_gather(w_query, ("frames", "fsdp"), axis=0, tiled=True),
        lax.all_gather(w_key, ("frames", "fsdp"), axis=0, tiled=True),
        lax.all_gather(w_value, ("frames", "fsdp"), axis=0, tiled=True),
    )
    sliced = normed
    projected = tuple(
        (jnp.dot(sliced, piece_part, preferred_element_type=jnp.float32) for piece_part in pieces)
    )
    head_count = att_cols // HEAD_DIM
    queries = projected[0].astype(jnp.bfloat16).reshape(frame_count, head_count, HEAD_DIM)
    key_rows = projected[1].astype(jnp.bfloat16)
    value_rows = projected[2].astype(jnp.bfloat16)
    length = lengths[0]
    scale_factor = 1.0 / math.sqrt(HEAD_DIM)
    start_max = jnp.full((frame_count, head_count), NEG_FILL, jnp.float32)
    pieces = (
        lax.all_gather(key_rows, "frames", axis=0, tiled=True),
        lax.all_gather(value_rows, "frames", axis=0, tiled=True),
    )
    key_block = pieces[0].reshape(-1, head_count, HEAD_DIM)
    value_block = pieces[1].reshape(-1, head_count, HEAD_DIM)
    block_rows = key_block.shape[0]
    scores = (
        jnp.einsum("qhd,khd->qhk", queries, key_block, preferred_element_type=jnp.float32)
        * scale_factor
    )
    valid = jnp.arange(block_rows, dtype=jnp.int32) < length
    masked = jnp.where(valid, scores, NEG_FILL)
    new_max = jnp.maximum(start_max, jnp.max(masked, axis=2))
    expo = jnp.where(valid, jnp.exp(masked - new_max[:, :, None]), 0.0)
    new_sum = jnp.sum(expo, axis=2)
    block_acc = jnp.einsum(
        "qhk,khd->qhd", expo.astype(jnp.bfloat16), value_block, preferred_element_type=jnp.float32
    )
    context = (block_acc / new_sum[:, :, None]).reshape(frame_count, att_cols).astype(jnp.bfloat16)
    partial_value = jnp.dot(
        context,
        lax.all_gather(w_out, ("frames", "fsdp"), axis=1, tiled=True),
        preferred_element_type=jnp.float32,
    )
    total = lax.psum(partial_value.astype(jnp.bfloat16), "heads").astype(jnp.float32)
    stream_full = (full_rows.astype(jnp.float32) + total).astype(jnp.bfloat16)
    stream_own = lax.dynamic_slice_in_dim(stream_full, own_start, half_width, 1)
    normed_two = layer_norm(stream_full).astype(jnp.bfloat16)
    channels = w_glu.shape[2]
    sliced = normed_two
    glu_pre = jnp.einsum(
        "td,dgc->tgc",
        sliced,
        lax.all_gather(w_glu, "fsdp", axis=0, tiled=True),
        preferred_element_type=jnp.float32,
    )
    positions = lax.axis_index("frames") * frame_count + jnp.arange(frame_count, dtype=jnp.int32)
    live = positions < length
    gated = jnp.where(
        live[:, None], glu_pre[:, 0, :] * jax.nn.sigmoid(glu_pre[:, 1, :]), 0.0
    ).astype(jnp.bfloat16)
    padded = padded_2(gated, (("frames", 0),), KERNEL // 2)
    depth = jnp.zeros((frame_count, channels), jnp.float32)
    for tap_index in range(KERNEL):
        depth = depth + padded[tap_index : tap_index + frame_count].astype(jnp.float32) * dw_kernel[
            tap_index
        ].astype(jnp.float32)
    hidden = (depth * jax.nn.sigmoid(depth)).astype(jnp.bfloat16)
    conv_part = jnp.dot(
        hidden, lax.all_gather(w_pw, "fsdp", axis=1, tiled=True), preferred_element_type=jnp.float32
    )
    conv_half = lax.psum_scatter(
        conv_part.astype(jnp.bfloat16), "heads", scatter_dimension=1, tiled=True
    ).astype(jnp.float32)
    result = (stream_own.astype(jnp.float32) + conv_half).astype(jnp.bfloat16)
    return result[None]


def solution(mesh):
    in_specs = (
        P(("groups", "fsdp"), "frames", "heads"),
        P(("groups", "fsdp")),
        P(("frames", "fsdp"), "heads"),
        P(("frames", "fsdp"), "heads"),
        P(("frames", "fsdp"), "heads"),
        P("heads", ("frames", "fsdp")),
        P("fsdp", None, "heads"),
        P(None, "heads"),
        P("heads", "fsdp"),
    )
    out_specs = P(("groups", "fsdp"), "frames", "heads")
    return jax.shard_map(shards, mesh=mesh, in_specs=in_specs, out_specs=out_specs, check_vma=False)
```

profile of v0, /device:TPU:0, one launch (start us, length us, event | category | flops | bytes accessed | tf_op | source)
XLA Modules:
  0.0 308.3 jit_solution(13441506892905612474)
XLA Ops:
  7.4 0.7 all-gather.9.cloned.1.call-update
  8.1 0.7 all-gather.11.cloned.1.call-update
  8.9 0.7 all-gather.7.cloned.1.call-update
  9.6 0.5 all-gather.13.cloned.1.call-update
  10.2 2.5 all_gather.27
  12.9 0.3 fusion.13
  13.9 40.3 %all-gather.9.cloned.1.call-done = bf16[1536,384]{1,0:T(8,128)(2,1)} async-done(((bf16[192,384]{1,0:T(8,128)(2,1)}), bf16[1536,384]{1,0:T(8,128)(2,1)}) %all-gather.9.cloned.1.call-update) | async-done | bytes 1179664 | tf_op jit(solution)/shard_map/all_gather | solution.py:50
  54.2 1.8 convolution_convert_fusion.3
  56.0 18.1 %all_gather.31 = bf16[768,384]{1,0:T(8,128)(2,1)S(1)} all-gather(bf16[192,384]{1,0:T(8,128)(2,1)S(1)} %convolution_convert_fusion.3), channel_id=1, replica_groups=mesh['groups'=2,'frames'=4,'fsdp'=2,'heads'=2] {'frames'}, dimensions={0}, use_global_device_ids=true | all-gather | bytes 737280 | tf_op jit(solution)/shard_map/all_gather | solution.py:65
  74.4 22.6 %all-gather.11.cloned.1.call-done = bf16[1536,384]{1,0:T(8,128)(2,1)} async-done(((bf16[192,384]{1,0:T(8,128)(2,1)}), bf16[1536,384]{1,0:T(8,128)(2,1)}) %all-gather.11.cloned.1.call-update) | async-done | bytes 1179664 | tf_op jit(solution)/shard_map/all_gather | solution.py:49
  97.0 1.8 convolution_convert_fusion.2
  98.9 40.1 %all-gather.7.cloned.1.call-done = bf16[1536,384]{1,0:T(8,128)(2,1)} async-done(((bf16[192,384]{1,0:T(8,128)(2,1)}), bf16[1536,384]{1,0:T(8,128)(2,1)}) %all-gather.7.cloned.1.call-update) | async-done | bytes 1179664 | tf_op jit(solution)/shard_map/all_gather | solution.py:51
  139.0 1.8 convolution_convert_fusion.4
  140.8 18.1 %all_gather.29 = bf16[768,384]{1,0:T(8,128)(2,1)S(1)} all-gather(bf16[192,384]{1,0:T(8,128)(2,1)S(1)} %convolution_convert_fusion.4), channel_id=1, replica_groups=mesh['groups'=2,'frames'=4,'fsdp'=2,'heads'=2] {'frames'}, dimensions={0}, use_global_device_ids=true | all-gather | bytes 737280 | tf_op jit(solution)/shard_map/all_gather | solution.py:66
  159.2 0.6 bitcast_reduce_fusion
  159.7 0.7 fusion.2
  160.5 0.8 fusion.22
  161.3 20.5 %all-gather.13.cloned.1.call-done = bf16[384,1536]{0,1:T(8,128)(2,1)} async-done(((bf16[384,192]{0,1:T(8,128)(2,1)}), bf16[384,1536]{0,1:T(8,128)(2,1)}) %all-gather.13.cloned.1.call-update) | async-done | bytes 1179664 | tf_op jit(solution)/shard_map/all_gather | solution.py:86
  181.8 2.8 convolution_convert_fusion.1
  184.7 1.8 copy.17
  186.5 0.5 all-gather.17.cloned.1.call-update
  187.4 15.0 %all-reduce.2.cloned.1.call-done = bf16[192,1536]{1,0:T(8,128)(2,1)} async-done(((bf16[192,1536]{1,0:T(8,128)(2,1)}), bf16[192,1536]{1,0:T(8,128)(2,1)}) %all-reduce.2.cloned.1.call-update) | async-done | bytes 589840 | tf_op jit(solution)/shard_map/psum | solution.py:89
  202.4 1.3 convert_reduce_fusion
  203.7 0.3 fusion.11
  204.0 44.0 %all-gather.15.cloned.1.call-done = bf16[1536,2,768]{2,0,1:T(8,128)(2,1)} async-done(((bf16[768,2,768]{2,0,1:T(8,128)(2,1)}), bf16[1536,2,768]{2,0,1:T(8,128)(2,1)}) %all-gather.15.cloned.1.call-update) | async-done | bytes 4718608 | tf_op jit(solution)/shard_map/all_gather | solution.py:98
  248.0 3.5 %fusion.26 = f32[192,2,768]{2,0,1:T(8,128)S(1)} fusion(bf16[1536,2,768]{2,0,1:T(8,128)(2,1)} %all-gather.15.cloned.1.call-done, bf16[192,1536]{1,0:T(8,128)(2,1)S(1)} %get-tuple-element.37, f32[192]{0:T(256)S(1)} %add_rsqrt_fusion, f32[192]{0:T(256)S(1)} %broadcast_multiply_fusion), kind=kOutput, calls=%fused_computation.64 | convolution fusion | flops 907149312 | bytes 6489600 | tf_op jit(solution)/shard_map/td,dgc->tgc/dot_general | solution.py:95
  251.7 3.4 %collective-permute-start = (bf16[15,768]{1,0:T(8,128)(2,1)S(1)}, bf16[15,768]{1,0:T(8,128)(2,1)S(1)}, u32[]{:S(2)}, u32[]{:S(2)}) collective-permute-start(bf16[15,768]{1,0:T(8,128)(2,1)S(1)} %get-tuple-element.38), channel_id=1, source_target_pairs={{0,4},{4,8},{8,12},{1,5},{5,9},{9,13},{2,6},{6,10},{10,14},{3,7},{... | collective-permute-start | bytes 69128 | tf_op jit(solution)/shard_map/ppermute | solution.py:24
  255.1 1.3 collective-permute-start.1
  256.5 28.9 %all-gather.17.cloned.1.call-done = bf16[768,1536]{1,0:T(8,128)(2,1)} async-done(((bf16[768,768]{1,0:T(8,128)(2,1)}), bf16[768,1536]{1,0:T(8,128)(2,1)}) %all-gather.17.cloned.1.call-update) | async-done | bytes 2359312 | tf_op jit(solution)/shard_map/all_gather | solution.py:114
  285.4 5.5 %convolution_convert_fusion = bf16[192,1536]{1,0:T(8,128)(2,1)} fusion(bf16[768,1536]{1,0:T(8,128)(2,1)} %all-gather.17.cloned.1.call-done, bf16[192,768]{1,0:T(8,128)(2,1)S(1)} %fusion.36, bf16[15,768]{1,0:T(8,128)(2,1)S(1)} %collective-permute-done.1, bf16[15,768]{1,0:T(8,128)(2,1)S(1)} %collective-permute-done, f32[768]{0:T(1024)S(1)} %get-tuple-element.34, ...), kind=kOutput, calls=%fused_computation | convolution fusion | flops 480854016 | bytes 3385344 | tf_op jit(solution)/shard_map/dot_general | solution.py:113
  290.9 8.2 %reduce-scatter.2.cloned.1.call-done = bf16[192,768]{1,0:T(8,128)(2,1)} async-done(((bf16[192,1536]{1,0:T(8,128)(2,1)}), bf16[192,768]{1,0:T(8,128)(2,1)}) %reduce-scatter.2.cloned.1.call-update) | async-done | bytes 294928 | tf_op jit(solution)/shard_map/reduce_scatter | solution.py:116
  299.1 1.7 fusion.37
  (32 shorter events, 1.8 us)
Async XLA Ops:
  7.4 46.8 %all-gather.9.cloned.1.call-start = ((), (), s32[]{:S(2)}) async-start(), calls=%async_computation.2 | async-start | bytes 1327104 | tf_op jit(solution)/shard_map/all_gather | solution.py:50
  8.1 88.9 %all-gather.11.cloned.1.call-start = ((), (), s32[]{:S(2)}) async-start(), calls=%async_computation.3 | async-start | bytes 1327104 | tf_op jit(solution)/shard_map/all_gather | solution.py:49
  8.8 130.2 %all-gather.7.cloned.1.call-start = ((), (), s32[]{:S(2)}) async-start(), calls=%async_computation.1 | async-start | bytes 1327104 | tf_op jit(solution)/shard_map/all_gather | solution.py:51
  9.6 172.2 %all-gather.13.cloned.1.call-start = ((), (), s32[]{:S(2)}) async-start(), calls=%async_computation.4 | async-start | bytes 1327104 | tf_op jit(solution)/shard_map/all_gather | solution.py:86
  10.1 192.3 %all-reduce.2.cloned.1.call-start = ((), (), s32[]{:S(2)}) async-start(), calls=%async_computation.5 | async-start | bytes 1179648 | tf_op jit(solution)/shard_map/psum | solution.py:89
  181.8 2.9 copy-start
  184.6 63.4 %all-gather.15.cloned.1.call-start = ((), (), s32[]{:S(2)}) async-start(), calls=%async_computation.6 | async-start | bytes 7077888 | tf_op jit(solution)/shard_map/all_gather | solution.py:98
  186.5 0.8 copy-start.1
  186.5 99.0 %all-gather.17.cloned.1.call-start = ((), (), s32[]{:S(2)}) async-start(), calls=%async_computation.7 | async-start | bytes 3538944 | tf_op jit(solution)/shard_map/all_gather | solution.py:114
  187.1 112.1 %reduce-scatter.2.cloned.1.call-start = ((), (), s32[]{:S(2)}) async-start(), calls=%async_computation.8 | async-start | bytes 884736 | tf_op jit(solution)/shard_map/reduce_scatter | solution.py:116
  251.7 33.7 %collective-permute-start = (bf16[15,768]{1,0:T(8,128)(2,1)S(1)}, bf16[15,768]{1,0:T(8,128)(2,1)S(1)}, u32[]{:S(2)}, u32[]{:S(2)}) collective-permute-start(bf16[15,768]{1,0:T(8,128)(2,1)S(1)} %get-tuple-element.38), channel_id=1, source_target_pairs={{0,4},{4,8},{8,12},{1,5},{5,9},{9,13},{2,6},{6,10},{10,14},{3,7},{... | collective-permute-start | bytes 69128 | tf_op jit(solution)/shard_map/ppermute | solution.py:24
  255.1 30.4 %collective-permute-start.1 = (bf16[15,768]{1,0:T(8,128)(2,1)S(1)}, bf16[15,768]{1,0:T(8,128)(2,1)S(1)}, u32[]{:S(2)}, u32[]{:S(2)}) collective-permute-start(bf16[15,768]{1,0:T(8,128)(2,1)S(1)} %get-tuple-element.39), channel_id=1, source_target_pairs={{4,0},{8,4},{12,8},{5,1},{9,5},{13,9},{6,2},{10,6},{14,10},{7,3},{... | collective-permute-start | bytes 69128 | tf_op jit(solution)/shard_map/ppermute | solution.py:26
Sparse Core Ops, SparseCore 0:
  10.4 43.7 all-gather.8
  56.3 40.5 all-gather.10
  99.1 39.8 all-gather.6
  141.0 40.6 all-gather.12
  184.7 17.6 all-reduce.1
  291.1 8.0 reduce-scatter.1
Sparse Core Ops, SparseCore 1:
  186.7 61.2 all-gather.14
  249.5 35.9 all-gather.16
where the time goes:
time: 309 us; the launch traced here: 308 us
  waiting for transfers between devices  223 us (72%)
  blocking collectives  38.8 us (13%)
  matrix products  18.5 us (6%)
  between operations  15.7 us (5%)
  other arithmetic  5.05 us (2%)
  starting transfers between devices  4.96 us (2%)
    all_gather x1, waiting for transfers between devices, shards(): lax.all_gather(w_glu, 'fsdp', axis=0, tiled=True)  44 us
    all_gather x1, waiting for transfers between devices, shards(): lax.all_gather(w_key, ('frames', 'fsdp'), axis=0, tiled=True)  40.3 us
    all_gather x1, waiting for transfers between devices, shards(): lax.all_gather(w_value, ('frames', 'fsdp'), axis=0, tiled=True)  40.1 us
    all_gather x1, waiting for transfers between devices, shards(): lax.all_gather(w_pw, 'fsdp', axis=1, tiled=True)  28.9 us
    all_gather x1, waiting for transfers between devices, shards(): lax.all_gather(w_query, ('frames', 'fsdp'), axis=0, tiled=True)  22.6 us
    all_gather x1, waiting for transfers between devices, shards(): lax.all_gather(w_out, ('frames', 'fsdp'), axis=1, tiled=True)  20.5 us
    all_gather x1, blocking collectives, shards(): lax.all_gather(key_rows, 'frames', axis=0, tiled=True)  18.1 us
    all_gather x1, blocking collectives, shards(): lax.all_gather(value_rows, 'frames', axis=0, tiled=True)  18.1 us
  transfers between devices with their start and end apart: 10, of which 8 were waited for; matrix products, arithmetic and copies ran while one was open for 5% of the time, Pallas kernels for 0%

commit v1 on v0

--- a/solution.py
+++ b/solution.py
@@ -1,8 +1,11 @@
+import functools
 import math
 
 import jax
 import jax.numpy as jnp
 from jax import lax
+from jax.experimental import pallas as pl
+from jax.experimental.pallas import tpu as pltpu
 from jax.sharding import PartitionSpec as P
 
 HEAD_DIM = 96
@@ -120,6 +123,354 @@
     return result[None]
 
 
+MESH = pl.DeviceIdType.MESH
+HALO = 16
+
+
+def block_kernel(
+    frames_ref, length_ref, shard_ref, glu_ref, taps_ref, pw_ref, out_ref,
+    full, packed, glu_all, pw_all, normed, qkv, kv_all, context,
+    part, part_in, stream, padded, edge, edge_in, hidden, conv, conv_in,
+    local_sem, send_sem, recv_sem,
+):
+    rows, half = frames_ref.shape
+    width = 2 * half
+    shard_rows = shard_ref.shape[0]
+    att = shard_ref.shape[1] // 4
+    g, f = lax.axis_index("groups"), lax.axis_index("frames")
+    s, h = lax.axis_index("fsdp"), lax.axis_index("heads")
+    ring = lax.axis_size("frames")
+    right, left = lax.rem(f + 1, ring), lax.rem(f + ring - 1, ring)
+    across = lax.rem(f + 2, ring)
+    peers = {
+        "right": {"frames": right}, "left": {"frames": left},
+        "x": {"fsdp": 1 - s}, "y": {"groups": 1 - g}, "core": {"heads": 1 - h},
+    }
+    names = {}
+
+    def copy(name, src, dst, to):
+        slot = names.setdefault(name, len(names))
+        return pltpu.make_async_remote_copy(
+            src_ref=src, dst_ref=dst, send_sem=send_sem.at[slot], recv_sem=recv_sem.at[slot],
+            device_id=peers[to], device_id_type=MESH,
+        )
+
+    barrier = pltpu.get_barrier_semaphore()
+    for to in peers:
+        pl.semaphore_signal(barrier, inc=1, device_id=peers[to], device_id_type=MESH)
+    pl.semaphore_wait(barrier, len(peers))
+
+    started = []
+
+    def start(c):
+        c.start()
+        started.append(c)
+        return c
+
+    def rows_at(index, first=0, count=shard_rows):
+        return pl.ds(pl.multiple_of(index * shard_rows + first, 16), count)
+
+    mid = shard_rows // 2
+    own_half = g * mid
+    columns = {"qkv": pl.ds(0, 3 * att), "out": pl.ds(3 * att, att)}
+
+    def at(kind, place, axis_s, first=0, count=shard_rows):
+        return packed.at[rows_at(place * 2 + axis_s, first, count), columns[kind]]
+
+    def own_src(kind, first=0, count=shard_rows):
+        return shard_ref.at[pl.ds(pl.multiple_of(first, 16), count), columns[kind]]
+
+    swap = start(copy("frames", frames_ref, full.at[h], "core"))
+    z_copies, x_copies, y_copies = {}, {}, {}
+
+    def z_first(kind):
+        for to in ("right", "left"):
+            z_copies[kind, to, 0] = start(
+                copy((kind, to, 0), own_src(kind), at(kind, f, s), to)
+            )
+
+    def x_send(kind, place_name, place):
+        src = own_src(kind, own_half, mid) if place_name == "own" else at(kind, place, s, own_half, mid)
+        x_copies[kind, place_name] = start(
+            copy((kind, "x", place_name), src, at(kind, place, s, own_half, mid), "x")
+        )
+
+    def y_forward(kind, place_name, place):
+        x_copies[kind, place_name].wait_recv()
+        block = at(kind, place, 1 - s, own_half, mid)
+        y_copies[kind, place_name] = start(copy((kind, "y", place_name), block, block, "y"))
+
+    def z_second(kind):
+        z_copies[kind, "right", 0].wait_recv()
+        top = at(kind, left, s, 0, mid)
+        z_copies[kind, "right", 1] = start(copy((kind, "right", 1), top, top, "right"))
+        x_send(kind, "left", left)
+        z_copies[kind, "left", 0].wait_recv()
+        low = at(kind, right, s, mid, mid)
+        z_copies[kind, "left", 1] = start(copy((kind, "left", 1), low, low, "left"))
+        x_send(kind, "right", right)
+
+    def z_last(kind):
+        z_copies[kind, "right", 1].wait_recv()
+        z_copies[kind, "left", 1].wait_recv()
+        x_send(kind, "across", across)
+
+    places = {"own": f, "left": left, "right": right, "across": across}
+
+    glu_rows = glu_ref.shape[0]
+    glu_part = glu_rows // 4
+    pw_rows = pw_ref.shape[0]
+    pw_part = pw_rows // 2
+    wide = {}
+
+    def glu_block(axis_s, piece):
+        return glu_all.at[axis_s, pl.ds(pl.multiple_of((g * 2 + piece) * glu_part, 16), glu_part), :]
+
+    def glu_send(piece):
+        src = glu_ref.at[pl.ds(pl.multiple_of((g * 2 + piece) * glu_part, 16), glu_part), :]
+        wide["glu", "x", piece] = start(copy(("glu", "x", piece), src, glu_block(s, piece), "x"))
+
+    def glu_forward(piece):
+        wide["glu", "x", piece].wait_recv()
+        block = glu_block(1 - s, piece)
+        wide["glu", "y", piece] = start(copy(("glu", "y", piece), block, block, "y"))
+
+    def pw_block(axis_s):
+        return pw_all.at[axis_s, pl.ds(pl.multiple_of(g * pw_part, 16), pw_part), :]
+
+    def pw_send():
+        src = pw_ref.at[pl.ds(pl.multiple_of(g * pw_part, 16), pw_part), :]
+        wide["pw", "x"] = start(copy(("pw", "x"), src, pw_block(s), "x"))
+
+    def pw_forward():
+        wide["pw", "x"].wait_recv()
+        block = pw_block(1 - s)
+        wide["pw", "y"] = start(copy(("pw", "y"), block, block, "y"))
+
+    def layer(read):
+        lo, hi = read(0), read(1)
+        mean = (jnp.sum(lo, axis=1, keepdims=True) + jnp.sum(hi, axis=1, keepdims=True)) / width
+        lo, hi = lo - mean, hi - mean
+        var = (jnp.sum(lo * lo, axis=1, keepdims=True) + jnp.sum(hi * hi, axis=1, keepdims=True)) / width
+        scale = lax.rsqrt(var + EPS)
+        normed[:, :half] = (lo * scale).astype(jnp.bfloat16)
+        normed[:, half:] = (hi * scale).astype(jnp.bfloat16)
+
+    z_first("qkv")
+    x_send("qkv", "own", f)
+    here = [
+        pltpu.make_async_copy(frames_ref, full.at[h], local_sem.at[0]),
+        pltpu.make_async_copy(shard_ref, packed.at[rows_at(f * 2 + s), :], local_sem.at[1]),
+        pltpu.make_async_copy(glu_ref, glu_all.at[s], local_sem.at[2]),
+        pltpu.make_async_copy(pw_ref, pw_all.at[s], local_sem.at[3]),
+    ]
+    for c in here:
+        c.start()
+    here[0].wait()
+    swap.wait_recv()
+    layer(lambda i: full[i].astype(jnp.float32))
+    y_forward("qkv", "own", f)
+    z_second("qkv")
+    z_first("out")
+    y_forward("qkv", "left", left)
+    y_forward("qkv", "right", right)
+    z_last("qkv")
+    glu_send(0)
+    y_forward("qkv", "across", across)
+    x_send("out", "own", f)
+    glu_send(1)
+    here[1].wait()
+    for name in places:
+        y_copies["qkv", name].wait_recv()
+
+    def project(tile):
+        cols = pl.ds(tile * att, att)
+        qkv[tile] = jnp.dot(
+            normed[...], packed[:, cols], preferred_element_type=jnp.float32
+        ).astype(jnp.bfloat16)
+
+    project(1)
+    project(2)
+
+    def kv_rows(place, first=0, count=rows):
+        return pl.ds(pl.multiple_of(place * rows + first, 16), count)
+
+    kv_all[0, kv_rows(f), :] = qkv[1]
+    kv_all[1, kv_rows(f), :] = qkv[2]
+    own_kv = kv_all.at[:, kv_rows(f), :]
+    kv = [start(copy(("kv", to), own_kv, own_kv, to)) for to in ("right", "left")]
+    project(0)
+    y_or = rows // 2
+    kv[0].wait_recv()
+    block = kv_all.at[:, kv_rows(left, 0, y_or), :]
+    kv.append(start(copy(("kv", "right", 1), block, block, "right")))
+    kv[1].wait_recv()
+    block = kv_all.at[:, kv_rows(right, y_or, y_or), :]
+    kv.append(start(copy(("kv", "left", 1), block, block, "left")))
+    z_second("out")
+    y_forward("out", "own", f)
+    glu_forward(0)
+    glu_forward(1)
+    z_last("out")
+    y_forward("out", "left", left)
+    y_forward("out", "right", right)
+    y_forward("out", "across", across)
+    pw_send()
+    kv[2].wait_recv()
+    kv[3].wait_recv()
+
+    length = length_ref[0]
+    total = kv_all.shape[1]
+    valid = lax.broadcasted_iota(jnp.int32, (1, total), 1) < length
+    column = lax.broadcasted_iota(jnp.int32, (1, att), 1)
+    scale_factor = 1.0 / math.sqrt(HEAD_DIM)
+    gathered = jnp.zeros((rows, att), jnp.float32)
+    for head in range(att // HEAD_DIM):
+        mine = (column >= head * HEAD_DIM) & (column < (head + 1) * HEAD_DIM)
+        query = jnp.where(mine, qkv[0].astype(jnp.float32), 0.0).astype(jnp.bfloat16)
+        scores = lax.dot_general(
+            query, kv_all[0], (((1,), (1,)), ((), ())), preferred_element_type=jnp.float32
+        ) * scale_factor
+        masked = jnp.where(valid, scores, NEG_FILL)
+        top = jnp.max(masked, axis=1, keepdims=True)
+        expo = jnp.where(valid, jnp.exp(masked - top), 0.0)
+        denom = jnp.sum(expo, axis=1, keepdims=True)
+        mixed = jnp.dot(
+            expo.astype(jnp.bfloat16), kv_all[1], preferred_element_type=jnp.float32
+        )
+        gathered = jnp.where(mine, mixed / denom, gathered)
+    context[...] = gathered.astype(jnp.bfloat16)
+
+    for name in places:
+        y_copies["out", name].wait_recv()
+    for i in range(2):
+        part[i] = lax.dot_general(
+            context[...], packed[i * half : (i + 1) * half, 3 * att :],
+            (((1,), (1,)), ((), ())), preferred_element_type=jnp.float32,
+        ).astype(jnp.bfloat16)
+    summed = start(copy("part", part, part_in, "core"))
+    pw_forward()
+    summed.wait_recv()
+    for i in range(2):
+        both = (part[i].astype(jnp.float32) + part_in[i].astype(jnp.float32)).astype(jnp.bfloat16)
+        stream[i] = (full[i].astype(jnp.float32) + both.astype(jnp.float32)).astype(jnp.bfloat16)
+    layer(lambda i: stream[i].astype(jnp.float32))
+
+    here[2].wait()
+    wide["glu", "y", 0].wait_recv()
+    wide["glu", "y", 1].wait_recv()
+    live = f * rows + lax.broadcasted_iota(jnp.int32, (rows, 1), 0) < length
+    tile_cols = 256
+
+    @pl.loop(0, half // tile_cols)
+    def _(tile):
+        first = pl.multiple_of(tile * tile_cols, tile_cols)
+        pre = []
+        for base in (0, half):
+            cols = pl.ds(base + first, tile_cols)
+            pre.append(
+                jnp.dot(normed[:, :half], glu_all[0, :, cols], preferred_element_type=jnp.float32)
+                + jnp.dot(normed[:, half:], glu_all[1, :, cols], preferred_element_type=jnp.float32)
+            )
+        gated = jnp.where(live, pre[0] * jax.nn.sigmoid(pre[1]), 0.0).astype(jnp.bfloat16)
+        cols = pl.ds(first, tile_cols)
+        edge[0, :, cols] = gated[:HALO]
+        edge[1, :, cols] = gated[rows - HALO :]
+        padded[pl.ds(HALO, rows), cols] = gated.astype(jnp.float32)
+
+    tail = start(copy("tail", edge.at[1], edge_in.at[0], "right"))
+    head = start(copy("head", edge.at[0], edge_in.at[1], "left"))
+    tail.wait_recv()
+    head.wait_recv()
+    has_left = jnp.where(f > 0, 1.0, 0.0)
+    has_right = jnp.where(f < ring - 1, 1.0, 0.0)
+    padded[:HALO, :] = edge_in[0].astype(jnp.float32) * has_left
+    padded[HALO + rows :, :] = edge_in[1].astype(jnp.float32) * has_right
+
+    lanes = 128
+    step_rows = 64
+
+    @pl.loop(0, half // lanes)
+    def _(tile):
+        cols = pl.ds(pl.multiple_of(tile * lanes, lanes), lanes)
+        taps = taps_ref[:, cols].astype(jnp.float32)
+        for first in range(0, rows, step_rows):
+            depth = jnp.zeros((step_rows, lanes), jnp.float32)
+            for tap in range(KERNEL):
+                at_row = first + tap + HALO - KERNEL // 2
+                depth = depth + padded[at_row : at_row + step_rows, cols] * taps[tap : tap + 1]
+            hidden[first : first + step_rows, cols] = (depth * jax.nn.sigmoid(depth)).astype(jnp.bfloat16)
+
+    here[3].wait()
+    wide["pw", "y"].wait_recv()
+    conv[1] = jnp.dot(
+        hidden[...], pw_all[1 - h], preferred_element_type=jnp.float32
+    ).astype(jnp.bfloat16)
+    given = start(copy("conv", conv.at[1], conv_in, "core"))
+    conv[0] = jnp.dot(
+        hidden[...], pw_all[h], preferred_element_type=jnp.float32
+    ).astype(jnp.bfloat16)
+    given.wait_recv()
+    both = (conv[0].astype(jnp.float32) + conv_in[...].astype(jnp.float32)).astype(jnp.bfloat16)
+    out_ref[...] = (stream[h].astype(jnp.float32) + both.astype(jnp.float32)).astype(jnp.bfloat16)
+    for c in started:
+        c.wait_send()
+
+
+def fused(frames_in, lengths, w_query, w_key, w_value, w_out, w_glu, dw_kernel, w_pw):
+    rows, half = frames_in.shape[1:]
+    att = w_query.shape[1]
+    width = 2 * half
+    ring = lax.axis_size("frames")
+    shard = jnp.concatenate([w_query, w_key, w_value, w_out.T], axis=1)
+    glu = w_glu.reshape(w_glu.shape[0], 2 * w_glu.shape[2])
+    bf16, f32 = jnp.bfloat16, jnp.float32
+    vmem = pl.BlockSpec(memory_space=pltpu.VMEM)
+    anywhere = pl.BlockSpec(memory_space=pl.ANY)
+    copies = 40
+    result = pl.pallas_call(
+        block_kernel,
+        out_shape=jax.ShapeDtypeStruct((rows, half), bf16),
+        in_specs=[anywhere, pl.BlockSpec(memory_space=pltpu.SMEM), anywhere, anywhere, vmem, anywhere],
+        out_specs=vmem,
+        scratch_shapes=[
+            pltpu.VMEM((2, rows, half), bf16),
+            pltpu.VMEM((width, 4 * att), bf16),
+            pltpu.VMEM((2,) + glu.shape, bf16),
+            pltpu.VMEM((2,) + w_pw.shape, bf16),
+            pltpu.VMEM((rows, width), bf16),
+            pltpu.VMEM((3, rows, att), bf16),
+            pltpu.VMEM((2, ring * rows, att), bf16),
+            pltpu.VMEM((rows, att), bf16),
+            pltpu.VMEM((2, rows, half), bf16),
+            pltpu.VMEM((2, rows, half), bf16),
+            pltpu.VMEM((2, rows, half), bf16),
+            pltpu.VMEM((rows + 2 * HALO, half), f32),
+            pltpu.VMEM((2, HALO, half), bf16),
+            pltpu.VMEM((2, HALO, half), bf16),
+            pltpu.VMEM((rows, half), bf16),
+            pltpu.VMEM((2, rows, half), bf16),
+            pltpu.VMEM((rows, half), bf16),
+            pltpu.SemaphoreType.DMA((4,)),
+            pltpu.SemaphoreType.DMA((copies,)),
+            pltpu.SemaphoreType.DMA((copies,)),
+        ],
+        compiler_params=pltpu.CompilerParams(
+            collective_id=0, has_side_effects=True, vmem_limit_bytes=52 * 2**20
+        ),
+        cost_estimate=pl.CostEstimate(
+            flops=2 * rows * width * (3 * att + 4 * half), bytes_accessed=2 * width * (4 * att + 6 * half),
+            transcendentals=rows * rows * ring * 4,
+        ),
+    )(frames_in[0], lengths, shard, glu, dw_kernel, w_pw)
+    return result[None]
+
+
+def fits(mesh):
+    sizes = dict(mesh.shape)
+    return sizes["groups"] == 2 and sizes["fsdp"] == 2 and sizes["heads"] == 2 and sizes["frames"] == 4
+
+
 def solution(mesh):
     in_specs = (
         P(("groups", "fsdp"), "frames", "heads"),
@@ -133,4 +484,5 @@
         P("heads", "fsdp"),
     )
     out_specs = P(("groups", "fsdp"), "frames", "heads")
-    return jax.shard_map(shards, mesh=mesh, in_specs=in_specs, out_specs=out_specs, check_vma=False)
+    body = fused if fits(mesh) else shards
+    return jax.shard_map(body, mesh=mesh, in_specs=in_specs, out_specs=out_specs, check_vma=False)

time: 309 us -> 116 us (0.38)
  waiting for transfers between devices: 223 us -> 0 us
  Pallas kernels: 0 us -> 110 us
  blocking collectives: 38.8 us -> 0 us
  matrix products: 18.5 us -> 0 us
  between operations: 15.7 us -> 0.68 us
  starting transfers between devices: 4.96 us -> 0 us
  other arithmetic: 5.05 us -> 1.17 us
    all_gather x6 -> x0, waiting for transfers between devices: 196 us -> none  [the longest x1 44 us: shards(): lax.all_gather(w_glu, 'fsdp', axis=0, tiled=True)]
    pallas_call x0 -> x1, Pallas kernels: none -> 110 us  [fused(): pl.pallas_call(block_kernel, out_shape=jax.ShapeDtypeStruct((rows, half),...]
    all_gather x3 -> x0, blocking collectives: 38.8 us -> none  [the longest x1 18.1 us: shards(): lax.all_gather(key_rows, 'frames', axis=0, tiled=True)]
    dot_general x8 -> x0, matrix products: 18.5 us -> none  [the longest x1 5.47 us: shards(): jnp.dot(hidden, lax.all_gather(w_pw, 'fsdp', axis=1, tiled=True), preferr...]
    psum x1 -> x0, waiting for transfers between devices: 15 us -> none  [shards(): lax.psum(partial_value.astype(jnp.bfloat16), 'heads').astype(jnp.float32)]
    reduce_scatter x1 -> x0, waiting for transfers between devices: 8.19 us -> none  [shards(): lax.psum_scatter(conv_part.astype(jnp.bfloat16), 'heads', scatter_dimensi...]
    ppermute x2 -> x0, starting transfers between devices: 4.68 us -> none  [the longest x1 3.39 us: padded_2(): lax.ppermute(tail, axis, [(i, (i + 1) % count) for i in range(ends)])]
    unnamed x8 -> x0, waiting for transfers between devices: 3.19 us -> none
  transfers between devices with their start and end apart: 10 -> 0, of which waited for: 8 -> 0; matrix products, arithmetic and copies ran while one was open for 5% -> 0% of each run, Pallas kernels for 0% -> 0%
where the time goes in v1:
time: 116 us
  Pallas kernels  110 us (95%)
  local copies, waits for them, and re-layouts  4.29 us (4%)
  other arithmetic  1.17 us (1%)
    pallas_call x1, Pallas kernels, fused(): pl.pallas_call(block_kernel, out_shape=jax.ShapeDtypeStruct((rows, half),...  110 us
    unnamed x6, local copies, waits for them, and re-layouts  4.29 us

profile of v1, /device:TPU:0, one launch (start us, length us, event | category | flops | bytes accessed | tf_op | source)
XLA Modules:
  0.0 116.1 jit_solution(1249212261765529244)
XLA Ops:
  0.7 1.2 %pad_maximum_fusion.shard_ref = bf16[192,1536]{1,0:T(8,128)(2,1)S(1)} fusion(bf16[192,384]{1,0:T(8,128)(2,1)} %bitcast.9, bf16[192,384]{1,0:T(8,128)(2,1)} %param.13, bf16[192,384]{1,0:T(8,128)(2,1)} %param.12, bf16[192,384]{1,0:T(8,128)(2,1)} %param.11), kind=kLoop, calls=%fused_computation | loop fusion | flops 2359296 | bytes 1179648 | tf_op jit(solution)/shard_map/concatenate | solution.py:425
  1.8 0.0 copy-start
  1.8 0.0 copy-start.1
  1.9 3.6 %copy.10 = bf16[96,8,2,768]{3,1,2,0:T(8,128)(2,1)} copy(bf16[96,8,2,768]{3,2,1,0:T(2,128)(2,1)} %bitcast.7) | data formatting | bytes 4718592
  5.4 0.0 copy-done
  5.4 0.0 copy-done.1
  5.4 109.9 %shard_map.91 = bf16[192,768]{1,0:T(8,128)(2,1)S(1)} custom-call(bf16[192,768]{1,0:T(8,128)(2,1)S(1)} %bitcast.6, s32[1]{0:T(128)S(6)} %copy.12.length_ref, bf16[192,1536]{1,0:T(8,128)(2,1)S(1)} %pad_maximum_fusion.shard_ref, bf16[768,1536]{1,0:T(8,128)(2,1)} %bitcast.8, bf16[31,768]{1,0:T(8,128)(2,1)S(1)} %copy-done.1, bf16[768,768]{1,0:T(8,128)(2,1)} %pw_ref.1), custom_call_target="tpu_custom_call" | custom-call | flops 2491416576 | bytes 18874368 | tf_op jit(solution)/shard_map/pallas_call | solution.py:431
  115.3 0.7 copy.13
Async XLA Ops:
  1.8 3.6 %copy-start = (bf16[1,192,768]{2,1,0:T(8,128)(2,1)S(1)}, bf16[1,192,768]{2,1,0:T(8,128)(2,1)}, u32[]{:S(2)}) copy-start(bf16[1,192,768]{2,1,0:T(8,128)(2,1)} %param.9) | copy-start | bytes 884740
  1.8 3.6 %copy-start.1 = (bf16[31,768]{1,0:T(8,128)(2,1)S(1)}, bf16[31,768]{1,0:T(8,128)(2,1)}, u32[]{:S(2)}) copy-start(bf16[31,768]{1,0:T(8,128)(2,1)} %taps_ref.1) | copy-start | bytes 142852

commit v2 on v1

--- a/solution.py
+++ b/solution.py
@@ -180,7 +180,39 @@
     def own_src(kind, first=0, count=shard_rows):
         return shard_ref.at[pl.ds(pl.multiple_of(first, 16), count), columns[kind]]
 
-    swap = start(copy("frames", frames_ref, full.at[h], "core"))
+    def frame_rows(place, first=0, count=rows):
+        return pl.ds(pl.multiple_of(place * rows + first, 16), count)
+
+    def frames_at(place, first=0, count=rows):
+        return full.at[h, frame_rows(place, first, count), :]
+
+    swaps = {"own": start(copy(("frames", "own"), frames_ref, frames_at(f), "core"))}
+    frame_copies = {}
+
+    def frames_first():
+        for to in ("right", "left"):
+            frame_copies[to, 0] = start(copy(("frames", to, 0), frames_ref, frames_at(f), to))
+
+    def frames_swap(name, place):
+        block = frames_at(place)
+        swaps[name] = start(copy(("frames", name), block, block, "core"))
+
+    def frames_second():
+        frame_mid = rows // 2
+        frame_copies["right", 0].wait_recv()
+        block = frames_at(left, 0, frame_mid)
+        frame_copies["right", 1] = start(copy(("frames", "right", 1), block, block, "right"))
+        frames_swap("left", left)
+        frame_copies["left", 0].wait_recv()
+        block = frames_at(right, frame_mid, frame_mid)
+        frame_copies["left", 1] = start(copy(("frames", "left", 1), block, block, "left"))
+        frames_swap("right", right)
+
+    def frames_last():
+        frame_copies["right", 1].wait_recv()
+        frame_copies["left", 1].wait_recv()
+        frames_swap("across", across)
+
     z_copies, x_copies, y_copies = {}, {}, {}
 
     def z_first(kind):
@@ -247,77 +279,74 @@
         block = pw_block(1 - s)
         wide["pw", "y"] = start(copy(("pw", "y"), block, block, "y"))
 
-    def layer(read):
+    def layer(read, at_rows):
         lo, hi = read(0), read(1)
         mean = (jnp.sum(lo, axis=1, keepdims=True) + jnp.sum(hi, axis=1, keepdims=True)) / width
         lo, hi = lo - mean, hi - mean
         var = (jnp.sum(lo * lo, axis=1, keepdims=True) + jnp.sum(hi * hi, axis=1, keepdims=True)) / width
         scale = lax.rsqrt(var + EPS)
-        normed[:, :half] = (lo * scale).astype(jnp.bfloat16)
-        normed[:, half:] = (hi * scale).astype(jnp.bfloat16)
+        normed[at_rows, :half] = (lo * scale).astype(jnp.bfloat16)
+        normed[at_rows, half:] = (hi * scale).astype(jnp.bfloat16)
 
     z_first("qkv")
     x_send("qkv", "own", f)
+    frames_first()
+    glu_send(0)
     here = [
-        pltpu.make_async_copy(frames_ref, full.at[h], local_sem.at[0]),
+        pltpu.make_async_copy(frames_ref, frames_at(f), local_sem.at[0]),
         pltpu.make_async_copy(shard_ref, packed.at[rows_at(f * 2 + s), :], local_sem.at[1]),
         pltpu.make_async_copy(glu_ref, glu_all.at[s], local_sem.at[2]),
         pltpu.make_async_copy(pw_ref, pw_all.at[s], local_sem.at[3]),
     ]
     for c in here:
         c.start()
+
+    def layer_block(name, place):
+        swaps[name].wait_recv()
+        where = frame_rows(place)
+        layer(lambda i: full[i, where, :].astype(jnp.float32), where)
+
     here[0].wait()
-    swap.wait_recv()
-    layer(lambda i: full[i].astype(jnp.float32))
+    layer_block("own", f)
     y_forward("qkv", "own", f)
     z_second("qkv")
+    frames_second()
     z_first("out")
     y_forward("qkv", "left", left)
     y_forward("qkv", "right", right)
+    glu_forward(0)
     z_last("qkv")
-    glu_send(0)
-    y_forward("qkv", "across", across)
     x_send("out", "own", f)
     glu_send(1)
+    layer_block("left", left)
+    layer_block("right", right)
+    y_forward("qkv", "across", across)
+    frames_last()
+    y_forward("out", "own", f)
+    layer_block("across", across)
     here[1].wait()
     for name in places:
         y_copies["qkv", name].wait_recv()
 
-    def project(tile):
-        cols = pl.ds(tile * att, att)
-        qkv[tile] = jnp.dot(
-            normed[...], packed[:, cols], preferred_element_type=jnp.float32
-        ).astype(jnp.bfloat16)
-
-    project(1)
-    project(2)
-
-    def kv_rows(place, first=0, count=rows):
-        return pl.ds(pl.multiple_of(place * rows + first, 16), count)
-
-    kv_all[0, kv_rows(f), :] = qkv[1]
-    kv_all[1, kv_rows(f), :] = qkv[2]
-    own_kv = kv_all.at[:, kv_rows(f), :]
-    kv = [start(copy(("kv", to), own_kv, own_kv, to)) for to in ("right", "left")]
-    project(0)
-    y_or = rows // 2
-    kv[0].wait_recv()
-    block = kv_all.at[:, kv_rows(left, 0, y_or), :]
-    kv.append(start(copy(("kv", "right", 1), block, block, "right")))
-    kv[1].wait_recv()
-    block = kv_all.at[:, kv_rows(right, y_or, y_or), :]
-    kv.append(start(copy(("kv", "left", 1), block, block, "left")))
+    @pl.loop(0, ring)
+    def _(place):
+        where = frame_rows(place)
+        for i in range(2):
+            kv_all[i, where, :] = jnp.dot(
+                normed[where, :], packed[:, (i + 1) * att : (i + 2) * att],
+                preferred_element_type=jnp.float32,
+            ).astype(jnp.bfloat16)
+
     z_second("out")
-    y_forward("out", "own", f)
-    glu_forward(0)
+    pw_send()
+    qkv[...] = jnp.dot(
+        normed[frame_rows(f), :], packed[:, :att], preferred_element_type=jnp.float32
+    ).astype(jnp.bfloat16)
     glu_forward(1)
-    z_last("out")
+
     y_forward("out", "left", left)
     y_forward("out", "right", right)
-    y_forward("out", "across", across)
-    pw_send()
-    kv[2].wait_recv()
-    kv[3].wait_recv()
+    z_last("out")
 
     length = length_ref[0]
     total = kv_all.shape[1]
@@ -327,7 +356,7 @@
     gathered = jnp.zeros((rows, att), jnp.float32)
     for head in range(att // HEAD_DIM):
         mine = (column >= head * HEAD_DIM) & (column < (head + 1) * HEAD_DIM)
-        query = jnp.where(mine, qkv[0].astype(jnp.float32), 0.0).astype(jnp.bfloat16)
+        query = jnp.where(mine, qkv[...].astype(jnp.float32), 0.0).astype(jnp.bfloat16)
         scores = lax.dot_general(
             query, kv_all[0], (((1,), (1,)), ((), ())), preferred_element_type=jnp.float32
         ) * scale_factor
@@ -341,6 +370,8 @@
         gathered = jnp.where(mine, mixed / denom, gathered)
     context[...] = gathered.astype(jnp.bfloat16)
 
+    y_forward("out", "across", across)
+    pw_forward()
     for name in places:
         y_copies["out", name].wait_recv()
     for i in range(2):
@@ -349,12 +380,11 @@
             (((1,), (1,)), ((), ())), preferred_element_type=jnp.float32,
         ).astype(jnp.bfloat16)
     summed = start(copy("part", part, part_in, "core"))
-    pw_forward()
     summed.wait_recv()
     for i in range(2):
         both = (part[i].astype(jnp.float32) + part_in[i].astype(jnp.float32)).astype(jnp.bfloat16)
-        stream[i] = (full[i].astype(jnp.float32) + both.astype(jnp.float32)).astype(jnp.bfloat16)
-    layer(lambda i: stream[i].astype(jnp.float32))
+        stream[i] = (full[i, frame_rows(f), :].astype(jnp.float32) + both.astype(jnp.float32)).astype(jnp.bfloat16)
+    layer(lambda i: stream[i].astype(jnp.float32), pl.ds(0, rows))
 
     here[2].wait()
     wide["glu", "y", 0].wait_recv()
@@ -369,8 +399,8 @@
         for base in (0, half):
             cols = pl.ds(base + first, tile_cols)
             pre.append(
-                jnp.dot(normed[:, :half], glu_all[0, :, cols], preferred_element_type=jnp.float32)
-                + jnp.dot(normed[:, half:], glu_all[1, :, cols], preferred_element_type=jnp.float32)
+                jnp.dot(normed[:rows, :half], glu_all[0, :, cols], preferred_element_type=jnp.float32)
+                + jnp.dot(normed[:rows, half:], glu_all[1, :, cols], preferred_element_type=jnp.float32)
             )
         gated = jnp.where(live, pre[0] * jax.nn.sigmoid(pre[1]), 0.0).astype(jnp.bfloat16)
         cols = pl.ds(first, tile_cols)
@@ -427,19 +457,19 @@
     bf16, f32 = jnp.bfloat16, jnp.float32
     vmem = pl.BlockSpec(memory_space=pltpu.VMEM)
     anywhere = pl.BlockSpec(memory_space=pl.ANY)
-    copies = 40
+    copies = 48
     result = pl.pallas_call(
         block_kernel,
         out_shape=jax.ShapeDtypeStruct((rows, half), bf16),
         in_specs=[anywhere, pl.BlockSpec(memory_space=pltpu.SMEM), anywhere, anywhere, vmem, anywhere],
         out_specs=vmem,
         scratch_shapes=[
-            pltpu.VMEM((2, rows, half), bf16),
+            pltpu.VMEM((2, ring * rows, half), bf16),
             pltpu.VMEM((width, 4 * att), bf16),
             pltpu.VMEM((2,) + glu.shape, bf16),
             pltpu.VMEM((2,) + w_pw.shape, bf16),
-            pltpu.VMEM((rows, width), bf16),
-            pltpu.VMEM((3, rows, att), bf16),
+            pltpu.VMEM((ring * rows, width), bf16),
+            pltpu.VMEM((rows, att), bf16),
             pltpu.VMEM((2, ring * rows, att), bf16),
             pltpu.VMEM((rows, att), bf16),
             pltpu.VMEM((2, rows, half), bf16),

time: 116 us -> 111 us (0.957)
  Pallas kernels: 110 us -> 105 us
    pallas_call x1, Pallas kernels: 110 us -> 105 us  [fused(): pl.pallas_call(block_kernel, out_shape=jax.ShapeDtypeStruct((rows, half),...]
where the time goes in v2:
time: 111 us
  Pallas kernels  105 us (95%)
  local copies, waits for them, and re-layouts  4.29 us (4%)
  other arithmetic  1.17 us (1%)
    pallas_call x1, Pallas kernels, fused(): pl.pallas_call(block_kernel, out_shape=jax.ShapeDtypeStruct((rows, half),...  105 us
    unnamed x6, local copies, waits for them, and re-layouts  4.29 us

profile of v2, /device:TPU:0, one launch (start us, length us, event | category | flops | bytes accessed | tf_op | source)
XLA Modules:
  0.0 110.7 jit_solution(11949734187462246695)
XLA Ops:
  0.7 1.2 %pad_maximum_fusion.shard_ref = bf16[192,1536]{1,0:T(8,128)(2,1)S(1)} fusion(bf16[192,384]{1,0:T(8,128)(2,1)} %bitcast.9, bf16[192,384]{1,0:T(8,128)(2,1)} %param.13, bf16[192,384]{1,0:T(8,128)(2,1)} %param.12, bf16[192,384]{1,0:T(8,128)(2,1)} %param.11), kind=kLoop, calls=%fused_computation | loop fusion | flops 2359296 | bytes 1179648 | tf_op jit(solution)/shard_map/concatenate | solution.py:455
  1.8 0.0 copy-start
  1.8 0.0 copy-start.1
  1.9 3.6 %copy.10 = bf16[96,8,2,768]{3,1,2,0:T(8,128)(2,1)} copy(bf16[96,8,2,768]{3,2,1,0:T(2,128)(2,1)} %bitcast.7) | data formatting | bytes 4718592
  5.4 0.0 copy-done
  5.4 0.0 copy-done.1
  5.4 104.5 %shard_map.91 = bf16[192,768]{1,0:T(8,128)(2,1)S(1)} custom-call(bf16[192,768]{1,0:T(8,128)(2,1)S(1)} %bitcast.6, s32[1]{0:T(128)S(6)} %copy.12.length_ref, bf16[192,1536]{1,0:T(8,128)(2,1)S(1)} %pad_maximum_fusion.shard_ref, bf16[768,1536]{1,0:T(8,128)(2,1)} %bitcast.8, bf16[31,768]{1,0:T(8,128)(2,1)S(1)} %copy-done.1, bf16[768,768]{1,0:T(8,128)(2,1)} %pw_ref.1), custom_call_target="tpu_custom_call" | custom-call | flops 2491416576 | bytes 18874368 | tf_op jit(solution)/shard_map/pallas_call | solution.py:461
  109.9 0.7 copy.13
Async XLA Ops:
  1.8 3.6 %copy-start = (bf16[1,192,768]{2,1,0:T(8,128)(2,1)S(1)}, bf16[1,192,768]{2,1,0:T(8,128)(2,1)}, u32[]{:S(2)}) copy-start(bf16[1,192,768]{2,1,0:T(8,128)(2,1)} %param.9) | copy-start | bytes 884740
  1.8 3.6 %copy-start.1 = (bf16[31,768]{1,0:T(8,128)(2,1)S(1)}, bf16[31,768]{1,0:T(8,128)(2,1)}, u32[]{:S(2)}) copy-start(bf16[31,768]{1,0:T(8,128)(2,1)} %taps_ref.1) | copy-start | bytes 142852

commit v3 on v2

--- a/solution.py
+++ b/solution.py
@@ -252,7 +252,7 @@
     glu_rows = glu_ref.shape[0]
     glu_part = glu_rows // 4
     pw_rows = pw_ref.shape[0]
-    pw_part = pw_rows // 2
+    pw_part = pw_rows // 4
     wide = {}
 
     def glu_block(axis_s, piece):
@@ -267,17 +267,18 @@
         block = glu_block(1 - s, piece)
         wide["glu", "y", piece] = start(copy(("glu", "y", piece), block, block, "y"))
 
-    def pw_block(axis_s):
-        return pw_all.at[axis_s, pl.ds(pl.multiple_of(g * pw_part, 16), pw_part), :]
-
-    def pw_send():
-        src = pw_ref.at[pl.ds(pl.multiple_of(g * pw_part, 16), pw_part), :]
-        wide["pw", "x"] = start(copy(("pw", "x"), src, pw_block(s), "x"))
-
-    def pw_forward():
-        wide["pw", "x"].wait_recv()
-        block = pw_block(1 - s)
-        wide["pw", "y"] = start(copy(("pw", "y"), block, block, "y"))
+    def pw_rows_at(piece):
+        return pl.ds(pl.multiple_of((g * 2 + piece) * pw_part, 16), pw_part)
+
+    def pw_send(piece):
+        src = pw_ref.at[pw_rows_at(piece), :]
+        dst = pw_all.at[s, pw_rows_at(piece), :]
+        wide["pw", "x", piece] = start(copy(("pw", "x", piece), src, dst, "x"))
+
+    def pw_forward(piece):
+        wide["pw", "x", piece].wait_recv()
+        block = pw_all.at[1 - s, pw_rows_at(piece), :]
+        wide["pw", "y", piece] = start(copy(("pw", "y", piece), block, block, "y"))
 
     def layer(read, at_rows):
         lo, hi = read(0), read(1)
@@ -318,6 +319,8 @@
     z_last("qkv")
     x_send("out", "own", f)
     glu_send(1)
+    pw_send(0)
+    pw_send(1)
     layer_block("left", left)
     layer_block("right", right)
     y_forward("qkv", "across", across)
@@ -338,7 +341,6 @@
             ).astype(jnp.bfloat16)
 
     z_second("out")
-    pw_send()
     qkv[...] = jnp.dot(
         normed[frame_rows(f), :], packed[:, :att], preferred_element_type=jnp.float32
     ).astype(jnp.bfloat16)
@@ -346,6 +348,7 @@
 
     y_forward("out", "left", left)
     y_forward("out", "right", right)
+    pw_forward(0)
     z_last("out")
 
     length = length_ref[0]
@@ -371,7 +374,7 @@
     context[...] = gathered.astype(jnp.bfloat16)
 
     y_forward("out", "across", across)
-    pw_forward()
+    pw_forward(1)
     for name in places:
         y_copies["out", name].wait_recv()
     for i in range(2):
@@ -432,7 +435,8 @@
             hidden[first : first + step_rows, cols] = (depth * jax.nn.sigmoid(depth)).astype(jnp.bfloat16)
 
     here[3].wait()
-    wide["pw", "y"].wait_recv()
+    wide["pw", "y", 0].wait_recv()
+    wide["pw", "y", 1].wait_recv()
     conv[1] = jnp.dot(
         hidden[...], pw_all[1 - h], preferred_element_type=jnp.float32
     ).astype(jnp.bfloat16)

time: 111 us -> 117 us (1.054)
  Pallas kernels: 105 us -> 111 us
    pallas_call x1, Pallas kernels: 105 us -> 111 us  [fused(): pl.pallas_call(block_kernel, out_shape=jax.ShapeDtypeStruct((rows, half),...]
where the time goes in v3:
time: 117 us
  Pallas kernels  111 us (95%)
  local copies, waits for them, and re-layouts  4.29 us (4%)
  other arithmetic  1.17 us (1%)
    pallas_call x1, Pallas kernels, fused(): pl.pallas_call(block_kernel, out_shape=jax.ShapeDtypeStruct((rows, half),...  111 us
    unnamed x6, local copies, waits for them, and re-layouts  4.29 us

profile of v3, /device:TPU:0, one launch (start us, length us, event | category | flops | bytes accessed | tf_op | source)
XLA Modules:
  0.0 117.3 jit_solution(17418460629707699130)
XLA Ops:
  0.7 1.2 %pad_maximum_fusion.shard_ref = bf16[192,1536]{1,0:T(8,128)(2,1)S(1)} fusion(bf16[192,384]{1,0:T(8,128)(2,1)} %bitcast.9, bf16[192,384]{1,0:T(8,128)(2,1)} %param.13, bf16[192,384]{1,0:T(8,128)(2,1)} %param.12, bf16[192,384]{1,0:T(8,128)(2,1)} %param.11), kind=kLoop, calls=%fused_computation | loop fusion | flops 2359296 | bytes 1179648 | tf_op jit(solution)/shard_map/concatenate | solution.py:459
  1.8 0.0 copy-start
  1.8 0.0 copy-start.1
  1.9 3.6 %copy.10 = bf16[96,8,2,768]{3,1,2,0:T(8,128)(2,1)} copy(bf16[96,8,2,768]{3,2,1,0:T(2,128)(2,1)} %bitcast.7) | data formatting | bytes 4718592
  5.4 0.0 copy-done
  5.4 0.0 copy-done.1
  5.4 111.2 %shard_map.91 = bf16[192,768]{1,0:T(8,128)(2,1)S(1)} custom-call(bf16[192,768]{1,0:T(8,128)(2,1)S(1)} %bitcast.6, s32[1]{0:T(128)S(6)} %copy.12.length_ref, bf16[192,1536]{1,0:T(8,128)(2,1)S(1)} %pad_maximum_fusion.shard_ref, bf16[768,1536]{1,0:T(8,128)(2,1)} %bitcast.8, bf16[31,768]{1,0:T(8,128)(2,1)S(1)} %copy-done.1, bf16[768,768]{1,0:T(8,128)(2,1)} %pw_ref.1), custom_call_target="tpu_custom_call" | custom-call | flops 2491416576 | bytes 18874368 | tf_op jit(solution)/shard_map/pallas_call | solution.py:465
  116.6 0.7 copy.13
Async XLA Ops:
  1.8 3.6 %copy-start = (bf16[1,192,768]{2,1,0:T(8,128)(2,1)S(1)}, bf16[1,192,768]{2,1,0:T(8,128)(2,1)}, u32[]{:S(2)}) copy-start(bf16[1,192,768]{2,1,0:T(8,128)(2,1)} %param.9) | copy-start | bytes 884740
  1.8 3.6 %copy-start.1 = (bf16[31,768]{1,0:T(8,128)(2,1)S(1)}, bf16[31,768]{1,0:T(8,128)(2,1)}, u32[]{:S(2)}) copy-start(bf16[31,768]{1,0:T(8,128)(2,1)} %taps_ref.1) | copy-start | bytes 142852

commit v4 on v3

--- a/solution.py
+++ b/solution.py
@@ -319,8 +319,6 @@
     z_last("qkv")
     x_send("out", "own", f)
     glu_send(1)
-    pw_send(0)
-    pw_send(1)
     layer_block("left", left)
     layer_block("right", right)
     y_forward("qkv", "across", across)
@@ -341,6 +339,7 @@
             ).astype(jnp.bfloat16)
 
     z_second("out")
+    pw_send(0)
     qkv[...] = jnp.dot(
         normed[frame_rows(f), :], packed[:, :att], preferred_element_type=jnp.float32
     ).astype(jnp.bfloat16)
@@ -348,8 +347,8 @@
 
     y_forward("out", "left", left)
     y_forward("out", "right", right)
-    pw_forward(0)
     z_last("out")
+    pw_send(1)
 
     length = length_ref[0]
     total = kv_all.shape[1]
@@ -374,7 +373,7 @@
     context[...] = gathered.astype(jnp.bfloat16)
 
     y_forward("out", "across", across)
-    pw_forward(1)
+    pw_forward(0)
     for name in places:
         y_copies["out", name].wait_recv()
     for i in range(2):
@@ -383,6 +382,7 @@
             (((1,), (1,)), ((), ())), preferred_element_type=jnp.float32,
         ).astype(jnp.bfloat16)
     summed = start(copy("part", part, part_in, "core"))
+    pw_forward(1)
     summed.wait_recv()
     for i in range(2):
         both = (part[i].astype(jnp.float32) + part_in[i].astype(jnp.float32)).astype(jnp.bfloat16)

time: 117 us -> 111 us (0.949)
  Pallas kernels: 111 us -> 105 us
    pallas_call x1, Pallas kernels: 111 us -> 105 us  [fused(): pl.pallas_call(block_kernel, out_shape=jax.ShapeDtypeStruct((rows, half),...]
where the time goes in v4:
time: 111 us
  Pallas kernels  105 us (95%)
  local copies, waits for them, and re-layouts  4.29 us (4%)
  other arithmetic  1.17 us (1%)
    pallas_call x1, Pallas kernels, fused(): pl.pallas_call(block_kernel, out_shape=jax.ShapeDtypeStruct((rows, half),...  105 us
    unnamed x6, local copies, waits for them, and re-layouts  4.29 us

profile of v4, /device:TPU:0, one launch (start us, length us, event | category | flops | bytes accessed | tf_op | source)
XLA Modules:
  0.0 110.9 jit_solution(13532487373633718951)
XLA Ops:
  0.7 1.2 %pad_maximum_fusion.shard_ref = bf16[192,1536]{1,0:T(8,128)(2,1)S(1)} fusion(bf16[192,384]{1,0:T(8,128)(2,1)} %bitcast.9, bf16[192,384]{1,0:T(8,128)(2,1)} %param.13, bf16[192,384]{1,0:T(8,128)(2,1)} %param.12, bf16[192,384]{1,0:T(8,128)(2,1)} %param.11), kind=kLoop, calls=%fused_computation | loop fusion | flops 2359296 | bytes 1179648 | tf_op jit(solution)/shard_map/concatenate | solution.py:459
  1.8 0.0 copy-start
  1.8 0.0 copy-start.1
  1.9 3.6 %copy.10 = bf16[96,8,2,768]{3,1,2,0:T(8,128)(2,1)} copy(bf16[96,8,2,768]{3,2,1,0:T(2,128)(2,1)} %bitcast.7) | data formatting | bytes 4718592
  5.4 0.0 copy-done
  5.4 0.0 copy-done.1
  5.4 104.7 %shard_map.91 = bf16[192,768]{1,0:T(8,128)(2,1)S(1)} custom-call(bf16[192,768]{1,0:T(8,128)(2,1)S(1)} %bitcast.6, s32[1]{0:T(128)S(6)} %copy.12.length_ref, bf16[192,1536]{1,0:T(8,128)(2,1)S(1)} %pad_maximum_fusion.shard_ref, bf16[768,1536]{1,0:T(8,128)(2,1)} %bitcast.8, bf16[31,768]{1,0:T(8,128)(2,1)S(1)} %copy-done.1, bf16[768,768]{1,0:T(8,128)(2,1)} %pw_ref.1), custom_call_target="tpu_custom_call" | custom-call | flops 2491416576 | bytes 18874368 | tf_op jit(solution)/shard_map/pallas_call | solution.py:465
  110.1 0.7 copy.13
Async XLA Ops:
  1.8 3.6 %copy-start = (bf16[1,192,768]{2,1,0:T(8,128)(2,1)S(1)}, bf16[1,192,768]{2,1,0:T(8,128)(2,1)}, u32[]{:S(2)}) copy-start(bf16[1,192,768]{2,1,0:T(8,128)(2,1)} %param.9) | copy-start | bytes 884740
  1.8 3.6 %copy-start.1 = (bf16[31,768]{1,0:T(8,128)(2,1)S(1)}, bf16[31,768]{1,0:T(8,128)(2,1)}, u32[]{:S(2)}) copy-start(bf16[31,768]{1,0:T(8,128)(2,1)} %taps_ref.1) | copy-start | bytes 142852

commit v5 on v4

--- a/solution.py
+++ b/solution.py
@@ -291,7 +291,6 @@
 
     z_first("qkv")
     x_send("qkv", "own", f)
-    frames_first()
     glu_send(0)
     here = [
         pltpu.make_async_copy(frames_ref, frames_at(f), local_sem.at[0]),
@@ -311,12 +310,13 @@
     layer_block("own", f)
     y_forward("qkv", "own", f)
     z_second("qkv")
+    frames_first()
+    y_forward("qkv", "left", left)
+    y_forward("qkv", "right", right)
+    z_last("qkv")
+    glu_forward(0)
     frames_second()
     z_first("out")
-    y_forward("qkv", "left", left)
-    y_forward("qkv", "right", right)
-    glu_forward(0)
-    z_last("qkv")
     x_send("out", "own", f)
     glu_send(1)
     layer_block("left", left)

time: 111 us -> 105 us (0.946)
  Pallas kernels: 105 us -> 98.6 us
    pallas_call x1, Pallas kernels: 105 us -> 98.6 us  [fused(): pl.pallas_call(block_kernel, out_shape=jax.ShapeDtypeStruct((rows, half),...]
where the time goes in v5:
time: 105 us
  Pallas kernels  98.6 us (94%)
  local copies, waits for them, and re-layouts  4.29 us (4%)
  other arithmetic  1.17 us (1%)
    pallas_call x1, Pallas kernels, fused(): pl.pallas_call(block_kernel, out_shape=jax.ShapeDtypeStruct((rows, half),...  98.6 us
    unnamed x6, local copies, waits for them, and re-layouts  4.29 us

profile of v5, /device:TPU:0, one launch (start us, length us, event | category | flops | bytes accessed | tf_op | source)
XLA Modules:
  0.0 104.7 jit_solution(3308432314817690739)
XLA Ops:
  0.7 1.2 %pad_maximum_fusion.shard_ref = bf16[192,1536]{1,0:T(8,128)(2,1)S(1)} fusion(bf16[192,384]{1,0:T(8,128)(2,1)} %bitcast.9, bf16[192,384]{1,0:T(8,128)(2,1)} %param.13, bf16[192,384]{1,0:T(8,128)(2,1)} %param.12, bf16[192,384]{1,0:T(8,128)(2,1)} %param.11), kind=kLoop, calls=%fused_computation | loop fusion | flops 2359296 | bytes 1179648 | tf_op jit(solution)/shard_map/concatenate | solution.py:459
  1.8 0.0 copy-start
  1.8 0.0 copy-start.1
  1.9 3.6 %copy.10 = bf16[96,8,2,768]{3,1,2,0:T(8,128)(2,1)} copy(bf16[96,8,2,768]{3,2,1,0:T(2,128)(2,1)} %bitcast.7) | data formatting | bytes 4718592
  5.4 0.0 copy-done
  5.4 0.0 copy-done.1
  5.4 98.6 %shard_map.91 = bf16[192,768]{1,0:T(8,128)(2,1)S(1)} custom-call(bf16[192,768]{1,0:T(8,128)(2,1)S(1)} %bitcast.6, s32[1]{0:T(128)S(6)} %copy.12.length_ref, bf16[192,1536]{1,0:T(8,128)(2,1)S(1)} %pad_maximum_fusion.shard_ref, bf16[768,1536]{1,0:T(8,128)(2,1)} %bitcast.8, bf16[31,768]{1,0:T(8,128)(2,1)S(1)} %copy-done.1, bf16[768,768]{1,0:T(8,128)(2,1)} %pw_ref.1), custom_call_target="tpu_custom_call" | custom-call | flops 2491416576 | bytes 18874368 | tf_op jit(solution)/shard_map/pallas_call | solution.py:465
  104.0 0.7 copy.13
Async XLA Ops:
  1.8 3.6 %copy-start = (bf16[1,192,768]{2,1,0:T(8,128)(2,1)S(1)}, bf16[1,192,768]{2,1,0:T(8,128)(2,1)}, u32[]{:S(2)}) copy-start(bf16[1,192,768]{2,1,0:T(8,128)(2,1)} %param.9) | copy-start | bytes 884740
  1.8 3.6 %copy-start.1 = (bf16[31,768]{1,0:T(8,128)(2,1)S(1)}, bf16[31,768]{1,0:T(8,128)(2,1)}, u32[]{:S(2)}) copy-start(bf16[31,768]{1,0:T(8,128)(2,1)} %taps_ref.1) | copy-start | bytes 142852
